TPU v7x, 256 devices: a whole 4x4x8 slice. The times are simulated.
256 devices in a mesh: brick: 32 (over z_hi, x, core), view: 8 (over y, z_lo).
Axes of the slice: x: 4, y: 4, z: 8 (z_hi: 4, z_lo: 2; z = z_hi * 2 + z_lo), core: 2. Of those that a mesh axis runs over, the one named last changes fastest.
Arguments:
- estimate: float32 [256, 64, 512], P('brick'), may hold values from 0.5 to 2
- camera_blocks: bfloat16 [8, 512, 8, 2048], P('view', 'brick'), may hold values from 0.099609375 to 2
- block_lists: int32 [8, 32, 32, 2], P('view'), may hold values from -1 to 15, as said below
- block_offsets: int32 [8, 512], P('view'), may hold values from 1 to 252, as said below
- psf_index: int32 [8, 64], P('view'), may hold values from 0 to 15
- psf_bank: float32 [8, 2, 16, 9], P('view'), may hold values from 0.03 to 0.3
Outputs:
- updated: float32 [256, 64, 512], P('brick')
Inputs may be any that keep to these rules, and one draw needn't show every extreme that they name: block_lists[v, d, s] names exactly the blocks of holder s that intersect brick d, each once; at most 2 of them, and 2 for some brick and holder. `block_offsets`: every block starts after its brick's first row by 1 to 4 rows.
All inputs are finite; a program needn't handle non-finite values.
Results may differ from a plain program's by a relative error of at most 0.0003.
Values may be sent and summed in bfloat16 or wider, within the bound.
A program may use at most 128 MiB of HBM per device.

v0:
```python
import jax
import jax.numpy as jnp
from jax import lax
from jax.sharding import PartitionSpec as P


def with_halo(cells, sides, width):
    for axis, dim in sides:
        count = lax.axis_size(axis)
        ends = count - 1
        head = lax.slice_in_dim(cells, 0, width, axis=dim)
        tail = lax.slice_in_dim(cells, cells.shape[dim] - width, cells.shape[dim], axis=dim)
        cells = jnp.concatenate(
            [
                lax.ppermute(tail, axis, [(i, (i + 1) % count) for i in range(ends)]),
                cells,
                lax.ppermute(head, axis, [((i + 1) % count, i) for i in range(ends)]),
            ],
            axis=dim,
        )
    return cells


def joined(value, axis, join):
    pieces = lax.all_gather(value, axis)
    head = pieces[0]
    tail = pieces[1:]
    running, _ = lax.scan(lambda running, slab: (join(running, slab), None), head, tail)
    return running


def blur_cols(field, kern, reverse):
    tap_count = kern.shape[1]
    radius = tap_count // 2
    width = field.shape[2]
    padded = jnp.pad(field, ((0, 0), (0, 0), (radius, radius)))
    result = None
    for offset in range(tap_count):
        begin_at = 2 * radius - offset if reverse else offset
        term = kern[:, offset][None, :, None] * padded[:, :, begin_at : begin_at + width]
        result = term if result is None else result + term
    return result


def blur_rows(padded, kern, reverse, rows):
    tap_count = kern.shape[1]
    radius = tap_count // 2
    result = None
    for offset in range(tap_count):
        begin_at = 2 * radius - offset if reverse else offset
        term = kern[:, offset][None, :, None] * padded[begin_at : begin_at + rows]
        result = term if result is None else result + term
    return result


def place_blocks(blocks, column_ids, row_starts, is_valid, start_x, rows_dev, depth, column_count):
    block_rows = blocks.shape[1]
    block_cols = column_count // 1
    local_rows = row_starts[:, None] + jnp.arange(block_rows, dtype=jnp.int32)[None, :] - start_x
    row_hit = (
        local_rows[:, :, None] == jnp.arange(rows_dev, dtype=jnp.int32)[None, None, :]
    ) & is_valid[:, None, None]
    colhot = column_ids[:, None] == jnp.arange(column_count, dtype=jnp.int32)[None, :]
    weight = (row_hit[:, :, :, None] & colhot[:, None, None, :]).astype(jnp.bfloat16)
    summed = jnp.einsum("sabc,saf->bcf", weight, blocks, preferred_element_type=jnp.float32)
    block_width = blocks.shape[2] // depth
    summed = summed.reshape(rows_dev, block_cols, depth, block_width)
    return summed.transpose(0, 2, 1, 3).reshape(rows_dev, depth, block_cols * block_width)


def multiply(first_value, second_value):
    return first_value * second_value


def shards(estimate, camera_blocks, block_lists, block_offsets, psf_index, psf_bank):
    rows_dev, depth, columns = estimate.shape
    tile_count = camera_blocks.shape[1]
    brick_here = lax.axis_index("brick")
    start_x = brick_here * rows_dev
    tap_count = psf_bank.shape[-1]
    radius = tap_count // 2
    kern_count = psf_bank.shape[2]
    kernel_pick = (
        psf_index[0][:, None] == jnp.arange(kern_count, dtype=jnp.int32)[None, :]
    ).astype(jnp.float32)
    kern_x = jnp.dot(kernel_pick, psf_bank[0, 0], precision=lax.Precision.HIGHEST)
    kern_y = jnp.dot(kernel_pick, psf_bank[0, 1], precision=lax.Precision.HIGHEST)
    offsets_view = block_offsets[0]
    gathered = lax.all_gather(camera_blocks, "brick", axis=1, tiled=True)
    count = gathered.shape[1]
    block_ids = jnp.arange(count, dtype=jnp.int32)
    measured = place_blocks(
        gathered[0],
        block_ids % tile_count,
        offsets_view,
        block_ids >= 0,
        start_x,
        rows_dev,
        depth,
        tile_count,
    )
    padded = with_halo(estimate, (("brick", 0),), radius)
    blurred = blur_rows(blur_cols(padded, kern_y, False), kern_x, False, rows_dev)
    ratio = measured / blurred
    padded_ratio = with_halo(ratio, (("brick", 0),), radius)
    correction = blur_rows(blur_cols(padded_ratio, kern_y, True), kern_x, True, rows_dev)
    product = joined(correction, "view", multiply)
    return estimate * product


def solution(mesh):
    placed = (
        P("brick", None, None),
        P("view", "brick", None, None),
        P("view", None, None, None),
        P("view", None),
        P("view", None),
        P("view", None, None, None),
    )
    return jax.shard_map(
        shards, mesh=mesh, in_specs=placed, out_specs=P("brick", None, None), check_vma=False
    )
```

profile of v0, /device:TPU:1, one launch (start us, length us, event | category | flops | bytes accessed | tf_op | source)
XLA Modules:
  0.0 433.1 jit_solution(10102572551987792969)
XLA Ops:
  7.3 2.1 fusion.49
  9.4 4.5 %collective-permute-start = (f32[4,64,512]{2,1,0:T(8,128)S(1)}, f32[4,64,512]{2,1,0:T(8,128)}, u32[]{:S(2)}, u32[]{:S(2)}) collective-permute-start(f32[4,64,512]{2,1,0:T(8,128)S(1)} %get-tuple-element.34), channel_id=1, source_target_pairs={{0,8},{8,16},{16,24},{24,32},{32,40},{40,48},{48,56},{56,64},{64,7... | collective-permute-start | bytes 1572872 | tf_op jit(solution)/shard_map/ppermute | solution.py:15
  13.9 2.7 collective-permute-start.1
  19.4 1.8 copy.23
  22.7 2.1 collective-permute-done.1
  24.7 2.4 copy.24
  27.1 1.7 pad_maximum_fusion
  28.8 6.2 %multiply_add_fusion.1 = f32[16,64,512]{1,2,0:T(8,128)} fusion(f32[16,64,512]{1,2,0:T(8,128)S(1)} %pad_maximum_fusion, f32[64]{0:T(128)S(1)} %get-tuple-element.48, f32[64]{0:T(128)S(1)} %get-tuple-element.49, f32[64]{0:T(128)S(1)} %get-tuple-element.50, f32[64]{0:T(128)S(1)} %get-tuple-element.51, f32[64]{0:T(128)S(1)} %get-tuple-element.52, ...), kind=kLoop, calls=%fused_computation.15 | loop fusion | flops 8912896 | bytes 4196608 | tf_op jit(solution)/shard_map/add | solution.py:41
  35.0 95.8 %all-gather.4.cloned.1.call-done = bf16[1,512,8,2048]{3,2,0,1:T(8,128)(2,1)} async-done(((bf16[1,16,8,2048]{3,2,0,1:T(8,128)(2,1)}), bf16[1,512,8,2048]{3,2,0,1:T(8,128)(2,1)}) %all-gather.4.cloned.1.call-update) | async-done | bytes 16777232 | tf_op jit(solution)/shard_map/all_gather | solution.py:89
  130.8 25.6 %copy.19 = bf16[1,512,8,2048]{1,2,3,0:T(8,128)(2,1)} copy(bf16[1,512,8,2048]{3,2,0,1:T(8,128)(2,1)} %all-gather.4.cloned.1.call-done) | data formatting | bytes 33554432 | tf_op jit(solution)/shard_map/all_gather | solution.py:89
  156.4 29.9 %fusion.32 = f32[8,64,16,32]{1,2,3,0:T(8,128)S(1)} fusion(bf16[64,32,8,512]{3,2,1,0:T(8,128)(2,1)} %bitcast.75, pred[512,16]{0,1:T(8,128)(4,1)S(1)} %iota_compare_fusion.1, pred[512,8,8]{0,1,2:T(8,128)(4,1)S(1)} %iota_compare_fusion), kind=kOutput, calls=%fused_computation.61 | convolution fusion | flops 2148007936 | bytes 17866752 | tf_op jit(solution)/shard_map/sabc,saf->bcf/dot_general | solution.py:65
  188.4 1.7 fusion.22
  191.3 2.3 copy.26
  193.6 2.3 collective-permute-start.3
  197.1 3.4 collective-permute-start.2
  200.5 4.0 collective-permute-done.3
  206.9 2.4 copy.27
  209.2 1.7 pad_maximum_fusion.1
  210.9 5.3 %multiply_add_fusion = f32[16,64,512]{1,2,0:T(8,128)S(1)} fusion(f32[16,64,512]{1,2,0:T(8,128)S(1)} %pad_maximum_fusion.1, f32[64]{0:T(128)S(1)} %get-tuple-element.48, f32[64]{0:T(128)S(1)} %get-tuple-element.49, f32[64]{0:T(128)S(1)} %get-tuple-element.50, f32[64]{0:T(128)S(1)} %get-tuple-element.51, f32[64]{0:T(128)S(1)} %get-tuple-element.52, ...), kind=kLoop, calls=%fused_computation.6 | loop fusion | flops 8912896 | bytes 4196608 | tf_op jit(solution)/shard_map/add | solution.py:41
  217.5 1.6 copy.29
  219.1 187.4 %all-gather.6.cloned.1.call-done = f32[64,64,512]{2,1,0:T(8,128)} async-done(((f32[8,64,512]{2,1,0:T(8,128)}), f32[64,64,512]{2,1,0:T(8,128)}) %all-gather.6.cloned.1.call-update) | async-done | bytes 8388624 | tf_op jit(solution)/shard_map/all_gather | solution.py:25
  406.6 7.7 %slice.301 = f32[56,64,512]{2,1,0:T(8,128)} slice(f32[64,64,512]{2,1,0:T(8,128)} %all-gather.6.cloned.1.call-done), slice={[8:64], [0:64], [0:512]} | slice | bytes 14680064 | tf_op jit(solution)/shard_map/slice | solution.py:27
  414.2 10.7 %while.10 = (s32[]{:T(128)}, f32[8,64,512]{2,1,0:T(8,128)S(1)}, f32[7,8,64,512]{3,2,1,0:T(8,128)}, s32[]{:T(128)}) while((s32[]{:T(128)}, f32[8,64,512]{2,1,0:T(8,128)S(1)}, f32[7,8,64,512]{3,2,1,0:T(8,128)}, s32[]{:T(128)}) %tuple.46), condition=%wide.region_1.2_spmd, body=%wide.region_0.1_spmd.sunk | while | flops 262146 | bytes 3145793 | solution.py:28
  414.3 1.6 bitcast_multiply_fusion.2
  (38 shorter events, 23.4 us)
Async XLA Ops:
  6.5 14.7 %copy-start.2 = (s32[1,512]{1,0:T(1,128)S(1)}, s32[1,512]{1,0:T(1,128)}, u32[]{:S(2)}) copy-start(s32[1,512]{1,0:T(1,128)} %param.10) | copy-start | bytes 6148
  6.5 124.3 %all-gather.4.cloned.1.call-start = ((), (), s32[]{:S(2)}) async-start(), calls=%async_computation | async-start | bytes 17301504 | tf_op jit(solution)/shard_map/all_gather | solution.py:89
  7.3 399.3 %all-gather.6.cloned.1.call-start = ((), (), s32[]{:S(2)}) async-start(), calls=%async_computation.1 | async-start | bytes 9437184 | tf_op jit(solution)/shard_map/all_gather | solution.py:25
  9.4 11.9 %collective-permute-start = (f32[4,64,512]{2,1,0:T(8,128)S(1)}, f32[4,64,512]{2,1,0:T(8,128)}, u32[]{:S(2)}, u32[]{:S(2)}) collective-permute-start(f32[4,64,512]{2,1,0:T(8,128)S(1)} %get-tuple-element.34), channel_id=1, source_target_pairs={{0,8},{8,16},{16,24},{24,32},{32,40},{40,48},{48,56},{56,64},{64,7... | collective-permute-start | bytes 1572872 | tf_op jit(solution)/shard_map/ppermute | solution.py:15
  13.9 10.8 %collective-permute-start.1 = (f32[4,64,512]{2,1,0:T(8,128)}, f32[4,64,512]{2,1,0:T(8,128)}, u32[]{:S(2)}, u32[]{:S(2)}) collective-permute-start(f32[4,64,512]{2,1,0:T(8,128)} %get-tuple-element.35), channel_id=1, source_target_pairs={{8,0},{16,8},{24,16},{32,24},{40,32},{48,40},{56,48},{64,56},{72,6... | collective-permute-start | bytes 1572872 | tf_op jit(solution)/shard_map/ppermute | solution.py:17
  186.2 2.2 copy-start
  193.6 10.8 %collective-permute-start.3 = (f32[4,64,512]{2,1,0:T(8,128)}, f32[4,64,512]{2,1,0:T(8,128)}, u32[]{:S(2)}, u32[]{:S(2)}) collective-permute-start(f32[4,64,512]{2,1,0:T(8,128)} %copy.26), channel_id=1, source_target_pairs={{8,0},{16,8},{24,16},{32,24},{40,32},{48,40},{56,48},{64,56},{72,6... | collective-permute-start | bytes 1572872 | tf_op jit(solution)/shard_map/ppermute | solution.py:17
  197.1 9.8 %collective-permute-start.2 = (f32[4,64,512]{2,1,0:T(8,128)}, f32[4,64,512]{2,1,0:T(8,128)}, u32[]{:S(2)}, u32[]{:S(2)}) collective-permute-start(f32[4,64,512]{2,1,0:T(8,128)} %copy.25), channel_id=1, source_target_pairs={{0,8},{8,16},{16,24},{24,32},{32,40},{40,48},{48,56},{56,64},{64,7... | collective-permute-start | bytes 1572872 | tf_op jit(solution)/shard_map/ppermute | solution.py:15
  406.6 7.7 %slice-start = ((f32[64,64,512]{2,1,0:T(8,128)}), f32[8,64,512]{2,1,0:T(8,128)S(1)}, s32[]{:S(2)}) async-start(f32[64,64,512]{2,1,0:T(8,128)} %all-gather.6.cloned.1.call-done), calls=%async_computation.2 | async-start | bytes 2097152 | tf_op jit(solution)/shard_map/slice | solution.py:26
  414.2 10.7 %copy-start.1 = (f32[8,64,512]{2,1,0:T(8,128)S(1)}, f32[8,64,512]{2,1,0:T(8,128)}, u32[]{:S(2)}) copy-start(f32[8,64,512]{2,1,0:T(8,128)} %param.8) | copy-start | bytes 3145732
Sparse Core Ops, SparseCore 0:
  9.9 120.8 all-gather.3
  219.2 187.2 all-gather.5
where the time goes:
time: 435 us; the launch traced here: 433 us
  waiting for transfers between devices  291 us (67%)
  local copies, waits for them, and re-layouts  54 us (12%)
  matrix products  31.6 us (7%)
  other arithmetic  29.8 us (7%)
  between operations  13.6 us (3%)
  starting transfers between devices  13 us (3%)
    all_gather x1, waiting for transfers between devices, joined(): pieces = lax.all_gather(value, axis)  187 us
    all_gather x1, waiting for transfers between devices, shards(): gathered = lax.all_gather(camera_blocks, 'brick', axis=1, tiled=True)  95.8 us
    dot_general x1, matrix products, place_blocks(): jnp.einsum('sabc,saf->bcf', weight, blocks, preferred_element_type=jnp.fl...  29.9 us
    all_gather x1, local copies, waits for them, and re-layouts, shards(): gathered = lax.all_gather(camera_blocks, 'brick', axis=1, tiled=True)  25.6 us
    add x2, other arithmetic, blur_cols(): result = term if result is None else result + term  11.4 us
    mul x7, other arithmetic, multiply(): return first_value * second_value  10.6 us
  transfers between devices with their start and end apart: 6, of which 5 were waited for; matrix products, arithmetic and copies ran while one was open for 5% of the time, Pallas kernels for 0%

commit v1 on v0

--- a/solution.py
+++ b/solution.py
@@ -86,7 +86,15 @@
     kern_x = jnp.dot(kernel_pick, psf_bank[0, 0], precision=lax.Precision.HIGHEST)
     kern_y = jnp.dot(kernel_pick, psf_bank[0, 1], precision=lax.Precision.HIGHEST)
     offsets_view = block_offsets[0]
-    gathered = lax.all_gather(camera_blocks, "brick", axis=1, tiled=True)
+    gathered = jnp.concatenate(
+        jax.lax.all_to_all(
+            jnp.stack([camera_blocks for _ in range(jax.lax.axis_size("brick"))], 0),
+            axis_name="brick",
+            split_axis=0,
+            concat_axis=0,
+        ),
+        1,
+    )
     count = gathered.shape[1]
     block_ids = jnp.arange(count, dtype=jnp.int32)
     measured = place_blocks(

time: 435 us -> 715 us (1.64)
  waiting for transfers between devices: 291 us -> 554 us
  starting transfers between devices: 13 us -> 24.1 us
  local copies, waits for them, and re-layouts: 54 us -> 61.3 us
    all_to_all x0 -> x1, waiting for transfers between devices: none -> 253 us  [shards(): jax.lax.all_to_all(jnp.stack([camera_blocks for _ in range(jax.lax.axis_s...]
    all_gather x1 -> x0, waiting for transfers between devices: 95.8 us -> none  [shards(): gathered = lax.all_gather(camera_blocks, 'brick', axis=1, tiled=True)]
    ppermute x2, waiting for transfers between devices: 1.09 us -> 78.8 us  [with_halo(): lax.ppermute(tail, axis, [(i, (i + 1) % count) for i in range(ends)])]
    all_gather x1 -> x0, local copies, waits for them, and re-layouts: 25.6 us -> none  [shards(): gathered = lax.all_gather(camera_blocks, 'brick', axis=1, tiled=True)]
    dot_general x0 -> x1, local copies, waits for them, and re-layouts: none -> 25.6 us  [place_blocks(): jnp.einsum('sabc,saf->bcf', weight, blocks, preferred_element_type=jnp.fl...]
    all_gather x1, waiting for transfers between devices: 187 us -> 203 us  [joined(): pieces = lax.all_gather(value, axis)]
    ppermute x2, waiting for transfers between devices: 6.01 us -> 19.9 us  [with_halo(): lax.ppermute(head, axis, [((i + 1) % count, i) for i in range(ends)])]
    all_to_all x0 -> x1, starting transfers between devices: none -> 12.8 us  [shards(): jax.lax.all_to_all(jnp.stack([camera_blocks for _ in range(jax.lax.axis_s...]
  transfers between devices with their start and end apart: 6 -> 6, of which waited for: 5 -> 6; matrix products, arithmetic and copies ran while one was open for 5% -> 3% of each run, Pallas kernels for 0% -> 0%
where the time goes in v1:
time: 715 us; the launch traced here: 714 us
  waiting for transfers between devices  554 us (77%)
  local copies, waits for them, and re-layouts  61.3 us (9%)
  other arithmetic  30.3 us (4%)
  matrix products  30.3 us (4%)
  starting transfers between devices  24.1 us (3%)
  between operations  13.6 us (2%)
    all_to_all x1, waiting for transfers between devices, shards(): jax.lax.all_to_all(jnp.stack([camera_blocks for _ in range(jax.lax.axis_s...  253 us
    all_gather x1, waiting for transfers between devices, joined(): pieces = lax.all_gather(value, axis)  203 us
    ppermute x2, waiting for transfers between devices, with_halo(): lax.ppermute(tail, axis, [(i, (i + 1) % count) for i in range(ends)])  78.8 us
    dot_general x1, matrix products, place_blocks(): jnp.einsum('sabc,saf->bcf', weight, blocks, preferred_element_type=jnp.fl...  29.9 us
    dot_general x1, local copies, waits for them, and re-layouts, place_blocks(): jnp.einsum('sabc,saf->bcf', weight, blocks, preferred_element_type=jnp.fl...  25.6 us
    ppermute x2, waiting for transfers between devices, with_halo(): lax.ppermute(head, axis, [((i + 1) % count, i) for i in range(ends)])  19.9 us
  transfers between devices with their start and end apart: 6, of which 6 were waited for; matrix products, arithmetic and copies ran while one was open for 3% of the time, Pallas kernels for 0%

profile of v1, /device:TPU:1, one launch (start us, length us, event | category | flops | bytes accessed | tf_op | source)
XLA Modules:
  0.0 713.6 jit_solution(9467658894080975121)
XLA Ops:
  6.5 6.8 stack.2
  13.3 12.8 %all-to-all-start = ((bf16[32,1,16,8,2048]{4,3,2,1,0:T(8,128)(2,1)}), bf16[32,1,16,8,2048]{4,3,2,1,0:T(8,128)(2,1)}, u32[]{:S(2)}, u32[]{:S(2)}) async-start(bf16[32,1,16,8,2048]{4,3,2,1,0:T(8,128)(2,1)} %stack.2), calls=%async_computation | async-start | bytes 33554432 | tf_op jit(solution)/shard_map/all_to_all | solution.py:90
  27.3 3.5 collective-permute-start
  30.8 1.9 collective-permute-start.1
  34.1 76.8 %collective-permute-done = f32[4,64,512]{2,1,0:T(8,128)} collective-permute-done((f32[4,64,512]{2,1,0:T(8,128)}, f32[4,64,512]{2,1,0:T(8,128)}, u32[]{:S(2)}, u32[]{:S(2)}) %collective-permute-start) | collective-permute-done | bytes 524320 | tf_op jit(solution)/shard_map/ppermute | solution.py:15
  110.9 2.4 copy.31
  113.3 15.3 %collective-permute-done.1 = f32[4,64,512]{2,1,0:T(8,128)} collective-permute-done((f32[4,64,512]{2,1,0:T(8,128)}, f32[4,64,512]{2,1,0:T(8,128)}, u32[]{:S(2)}, u32[]{:S(2)}) %collective-permute-start.1) | collective-permute-done | bytes 524320 | tf_op jit(solution)/shard_map/ppermute | solution.py:17
  128.6 2.4 copy.33
  132.8 6.3 multiply_add_fusion.1
  139.2 252.6 %all-to-all-done = bf16[32,1,16,8,2048]{4,3,2,1,0:T(8,128)(2,1)} async-done(((bf16[32,1,16,8,2048]{4,3,2,1,0:T(8,128)(2,1)}), bf16[32,1,16,8,2048]{4,3,2,1,0:T(8,128)(2,1)}, u32[]{:S(2)}, u32[]{:S(2)}) %all-to-all-start) | async-done | bytes 16777248 | tf_op jit(solution)/shard_map/all_to_all | solution.py:90
  391.8 25.6 %copy.28 = bf16[2048,8,512]{2,1,0:T(8,128)(2,1)} copy(bf16[2048,8,512]{0,1,2:T(8,128)(2,1)} %bitcast.11) | data formatting | bytes 33554432 | tf_op jit(solution)/shard_map/sabc,saf->bcf/dot_general | solution.py:65
  417.3 29.9 %fusion.32 = f32[8,64,16,32]{1,2,3,0:T(8,128)S(1)} fusion(bf16[64,32,8,512]{3,2,1,0:T(8,128)(2,1)} %bitcast.74, pred[512,16]{0,1:T(8,128)(4,1)S(1)} %iota_compare_fusion.1, pred[512,8,8]{0,1,2:T(8,128)(4,1)S(1)} %iota_compare_fusion), kind=kOutput, calls=%fused_computation.61 | convolution fusion | flops 2148007936 | bytes 17866752 | tf_op jit(solution)/shard_map/sabc,saf->bcf/dot_general | solution.py:65
  452.6 2.3 copy.34
  455.0 3.9 collective-permute-start.2
  458.9 2.3 copy.35
  461.2 1.9 collective-permute-start.3
  463.1 1.9 collective-permute-done.2
  465.1 2.4 copy.36
  467.4 4.6 collective-permute-done.3
  472.0 2.4 copy.37
  476.3 5.3 multiply_add_fusion
  484.5 202.7 %all-gather.3.cloned.1.call-done = f32[64,64,512]{2,1,0:T(8,128)} async-done(((f32[8,64,512]{2,1,0:T(8,128)}), f32[64,64,512]{2,1,0:T(8,128)}) %all-gather.3.cloned.1.call-update) | async-done | bytes 8388624 | tf_op jit(solution)/shard_map/all_gather | solution.py:25
  687.2 7.7 %slice.301 = f32[56,64,512]{2,1,0:T(8,128)} slice(f32[64,64,512]{2,1,0:T(8,128)} %all-gather.3.cloned.1.call-done), slice={[8:64], [0:64], [0:512]} | slice | bytes 14680064 | tf_op jit(solution)/shard_map/slice | solution.py:27
  694.9 10.6 %while.10 = (s32[]{:T(128)}, f32[8,64,512]{2,1,0:T(8,128)S(1)}, f32[7,8,64,512]{3,2,1,0:T(8,128)}, s32[]{:T(128)}) while((s32[]{:T(128)}, f32[8,64,512]{2,1,0:T(8,128)S(1)}, f32[7,8,64,512]{3,2,1,0:T(8,128)}, s32[]{:T(128)}) %tuple.45), condition=%wide.region_1.2_spmd, body=%wide.region_0.1_spmd.sunk | while | flops 262146 | bytes 3145785 | solution.py:28
  (42 shorter events, 26.3 us)
Async XLA Ops:
  13.3 12.9 %copy-start.1 = (f32[8,64,512]{2,1,0:T(8,128)S(1)}, f32[8,64,512]{2,1,0:T(8,128)}, u32[]{:S(2)}) copy-start(f32[8,64,512]{2,1,0:T(8,128)} %param.8) | copy-start | bytes 3145732
  13.3 19.4 %copy-start.2 = (f32[1,2,16,9]{2,1,3,0:T(2,128)S(1)}, f32[1,2,16,9]{2,1,3,0:T(2,128)}, u32[]{:S(2)}) copy-start(f32[1,2,16,9]{2,1,3,0:T(2,128)} %param.12) | copy-start | bytes 3460
  13.3 19.6 %copy-start.4 = (s32[1,64]{1,0:T(1,128)S(1)}, s32[1,64]{1,0:T(1,128)}, u32[]{:S(2)}) copy-start(s32[1,64]{1,0:T(1,128)} %param.11) | copy-start | bytes 772
  13.3 378.5 %all-to-all-start = ((bf16[32,1,16,8,2048]{4,3,2,1,0:T(8,128)(2,1)}), bf16[32,1,16,8,2048]{4,3,2,1,0:T(8,128)(2,1)}, u32[]{:S(2)}, u32[]{:S(2)}) async-start(bf16[32,1,16,8,2048]{4,3,2,1,0:T(8,128)(2,1)} %stack.2), calls=%async_computation | async-start | bytes 33554432 | tf_op jit(solution)/shard_map/all_to_all | solution.py:90
  26.1 7.9 %copy-start.3 = (s32[1,512]{1,0:T(1,128)S(1)}, s32[1,512]{1,0:T(1,128)}, u32[]{:S(2)}) copy-start(s32[1,512]{1,0:T(1,128)} %param.10) | copy-start | bytes 6148
  26.1 661.1 %all-gather.3.cloned.1.call-start = ((), (), s32[]{:S(2)}) async-start(), calls=%async_computation.1 | async-start | bytes 9437184 | tf_op jit(solution)/shard_map/all_gather | solution.py:25
  27.3 83.6 %collective-permute-start = (f32[4,64,512]{2,1,0:T(8,128)}, f32[4,64,512]{2,1,0:T(8,128)}, u32[]{:S(2)}, u32[]{:S(2)}) collective-permute-start(f32[4,64,512]{2,1,0:T(8,128)} %get-tuple-element.37), channel_id=1, source_target_pairs={{0,8},{8,16},{16,24},{24,32},{32,40},{40,48},{48,56},{56,64},{64,7... | collective-permute-start | bytes 1572872 | tf_op jit(solution)/shard_map/ppermute | solution.py:15
  30.8 97.8 %collective-permute-start.1 = (f32[4,64,512]{2,1,0:T(8,128)}, f32[4,64,512]{2,1,0:T(8,128)}, u32[]{:S(2)}, u32[]{:S(2)}) collective-permute-start(f32[4,64,512]{2,1,0:T(8,128)} %get-tuple-element.38), channel_id=1, source_target_pairs={{8,0},{16,8},{24,16},{32,24},{40,32},{48,40},{56,48},{64,56},{72,6... | collective-permute-start | bytes 1572872 | tf_op jit(solution)/shard_map/ppermute | solution.py:17
  447.2 2.2 copy-start
  455.0 10.1 %collective-permute-start.2 = (f32[4,64,512]{2,1,0:T(8,128)}, f32[4,64,512]{2,1,0:T(8,128)}, u32[]{:S(2)}, u32[]{:S(2)}) collective-permute-start(f32[4,64,512]{2,1,0:T(8,128)} %copy.34), channel_id=1, source_target_pairs={{0,8},{8,16},{16,24},{24,32},{32,40},{40,48},{48,56},{56,64},{64,7... | collective-permute-start | bytes 1572872 | tf_op jit(solution)/shard_map/ppermute | solution.py:15
  461.2 10.8 %collective-permute-start.3 = (f32[4,64,512]{2,1,0:T(8,128)}, f32[4,64,512]{2,1,0:T(8,128)}, u32[]{:S(2)}, u32[]{:S(2)}) collective-permute-start(f32[4,64,512]{2,1,0:T(8,128)} %copy.35), channel_id=1, source_target_pairs={{8,0},{16,8},{24,16},{32,24},{40,32},{48,40},{56,48},{64,56},{72,6... | collective-permute-start | bytes 1572872 | tf_op jit(solution)/shard_map/ppermute | solution.py:17
  687.2 7.7 %slice-start = ((f32[64,64,512]{2,1,0:T(8,128)}), f32[8,64,512]{2,1,0:T(8,128)S(1)}, s32[]{:S(2)}) async-start(f32[64,64,512]{2,1,0:T(8,128)} %all-gather.3.cloned.1.call-done), calls=%async_computation.2 | async-start | bytes 2097152 | tf_op jit(solution)/shard_map/slice | solution.py:26
Sparse Core Ops, SparseCore 0:
  484.6 202.5 all-gather.2
